TPU v7x, 32 devices: a whole 2x2x4 slice. The times are simulated.
32 devices in a mesh: freq: 16 (over z, x, core), beam: 2 (over y).
Axes of the slice: x: 2, y: 2, z: 4, core: 2. Of those that a mesh axis runs over, the one named last changes fastest.
Arguments:
- voltages: bfloat16 [2, 4, 1024, 16, 256], P(None, 'beam', 'freq'), parts along dimension 1, may hold values from -6 to 6
- sub_delays: int32 [4096, 1024], P('freq'), may hold values from 0 to 31, as said below
- merge_tables: int32 [4, 3, 4096], P(None, None, 'freq'), may hold values from 0 to 255, as said below
Outputs:
- peak_values: float32 [4, 8, 4096], P('beam', None, 'freq'), parts along dimension 0
There are 2 independent parts, one for each index of `beam`. A program takes and returns all parts, laid end to end along the dimension named above; an argument that names none is the same for every part. Nothing has to cross between parts.
Inputs may be any that keep to these rules, and one draw needn't show every extreme that they name: `sub_delays`: every row has some channel with delay 32 - 1. `merge_tables`: for each level and each aligned block of 256 trials, rows 0 and 1 each hold a permutation of 0 to 255; row 2 holds delays of 0 to 63, and each such block has a delay of 63.
All inputs are finite; a program needn't handle non-finite values.
Results may differ from a plain program's by a relative error of at most 0.0003.
Values may be sent and summed in bfloat16 or wider, within the bound.
A program may use at most 128 MiB of HBM per device.

v0:
```python
import math

import jax
import jax.numpy as jnp
from jax import lax
from jax.sharding import PartitionSpec as P

TAPS = 4
WIDTHS = 8
SHIFTS = 32
CROSS_SHIFT = 64


epsilon = 1e-06


def from_partner(x, axis, distance):
    return lax.ppermute(x, axis, [(i, i ^ 1 << distance) for i in range(lax.axis_size(axis))])


def window_table(tap_count, upchan):
    length = tap_count * upchan
    positions = jnp.arange(length, dtype=jnp.float32)
    window = jnp.sinc((positions - (length - 1) / 2.0) / upchan)
    window = window * (0.5 - 0.5 * jnp.cos(2.0 * math.pi * (positions + 0.5) / length))
    window = window / jnp.sqrt(2.0 * jnp.sum(window * window))
    return window.reshape(tap_count, upchan)


def filter_power(volts):
    signal = volts.astype(jnp.float32)
    upchan = signal.shape[3]
    samples = signal.shape[4]
    window = window_table(TAPS, upchan)
    padded = jnp.pad(signal, ((0, 0), (0, 0), (0, 0), (0, 0), (TAPS - 1, 0)))
    filtered = jnp.zeros_like(signal)
    for offset in range(TAPS):
        filtered = (
            filtered
            + window[offset][:, None] * padded[..., TAPS - 1 - offset : TAPS - 1 - offset + samples]
        )
    phase = jnp.arange(upchan, dtype=jnp.float32)
    angle = 2.0 * math.pi * phase[:, None] * phase[None, :] / upchan
    cosine = jnp.cos(angle)
    sine_table = jnp.sin(angle)
    high = lax.Precision.HIGHEST
    real_part = jnp.einsum("km,bcmt->bckt", cosine, filtered[0], precision=high) + jnp.einsum(
        "km,bcmt->bckt", sine_table, filtered[1], precision=high
    )
    imag_part = jnp.einsum("km,bcmt->bckt", cosine, filtered[1], precision=high) - jnp.einsum(
        "km,bcmt->bckt", sine_table, filtered[0], precision=high
    )
    intensity = (real_part * real_part + imag_part * imag_part).astype(jnp.bfloat16)
    return intensity.reshape(signal.shape[1], signal.shape[2] * upchan, samples)


def delay_rows(series, delays, bit_count):
    samples = series.shape[-1]
    result = series
    for bit in range(bit_count):
        amount = 2**bit
        moved = jnp.pad(result[..., : samples - amount], ((0, 0), (0, 0), (amount, 0)))
        chosen = (delays // amount % 2 == 1)[None, :, None]
        result = jnp.where(chosen, moved, result)
    return result


def boxcar_peaks(series):
    samples = series.shape[-1]
    row_mean = jnp.mean(series, axis=-1, keepdims=True)
    centred = series - row_mean
    inv_scale = lax.rsqrt(jnp.mean(centred * centred, axis=-1, keepdims=True) + epsilon)
    boxcar = centred * inv_scale
    maxima = [jnp.max(boxcar, axis=-1)]
    span_now = 1
    for offset in range(1, WIDTHS):
        lagged = jnp.pad(boxcar[..., : samples - span_now], ((0, 0), (0, 0), (span_now, 0)))
        boxcar = boxcar + lagged
        span_now = span_now * 2
        maxima.append(jnp.max(boxcar, axis=-1) / math.sqrt(span_now))
    return jnp.stack(maxima, axis=1)


def local(voltages, sub_delays, merge_tables):
    freq_count = lax.axis_size("freq")
    coarse_local = voltages.shape[2]
    upchan = voltages.shape[3]
    samples = voltages.shape[4]
    per_source = coarse_local // freq_count
    row_count = sub_delays.shape[0]
    intensity = lax.all_to_all(
        filter_power(voltages), "freq", split_axis=1, concat_axis=1, tiled=True
    )
    delay_table = sub_delays.reshape(row_count, per_source, freq_count, upchan)
    delay_table = delay_table.transpose(0, 2, 1, 3).reshape(row_count, coarse_local * upchan)
    padded = jnp.pad(intensity, ((0, 0), (0, 0), (SHIFTS - 1, 0)))
    running = jnp.zeros((intensity.shape[0], row_count, samples), jnp.float32)
    for first_shift in range(0, SHIFTS, 4):
        onehot = jnp.stack(
            [delay_table == first_shift + offset for offset in range(4)], axis=1
        ).astype(jnp.bfloat16)
        shifted_block = jnp.stack(
            [
                padded[
                    :,
                    :,
                    SHIFTS - 1 - first_shift - offset : SHIFTS - 1 - first_shift - offset + samples,
                ]
                for offset in range(4)
            ],
            axis=1,
        )
        running = running + jnp.einsum(
            "rsc,bsct->brt", onehot, shifted_block, preferred_element_type=jnp.float32
        )
    merged = running
    position = lax.axis_index("freq")
    bit_count = max(CROSS_SHIFT - 1, 1).bit_length()
    for merge_level in range(freq_count.bit_length() - 1):
        partner = from_partner(merged, "freq", merge_level)
        upper_half = position // 2**merge_level % 2 == 1
        lower_source = jnp.where(upper_half, partner, merged)
        upper_source = jnp.where(upper_half, merged, partner)
        lower_term = lower_source[:, merge_tables[merge_level, 0], :]
        upper_term = upper_source[:, merge_tables[merge_level, 1], :]
        merged = lower_term + delay_rows(upper_term, merge_tables[merge_level, 2], bit_count)
    return boxcar_peaks(merged)


def solution(mesh):
    return jax.shard_map(
        local,
        mesh=mesh,
        in_specs=(P(None, "beam", "freq", None, None), P("freq", None), P(None, None, "freq")),
        out_specs=P("beam", None, "freq"),
        check_vma=False,
    )
```

profile of v0, /device:TPU:0, one launch (start us, length us, event | category | flops | bytes accessed | tf_op | source)
XLA Modules:
  0.0 211.6 jit_solution(5868118418627104868)
XLA Ops:
  0.7 4.2 %convert_element_type.64 = f32[2,2,64,16,256]{4,3,2,1,0:T(8,128)} convert(bf16[2,2,64,16,256]{4,3,2,1,0:T(8,128)(2,1)} %param.3) | non-fusion elementwise | flops 1048576 | bytes 6291456 | tf_op jit(solution)/shard_map/convert_element_type | solution.py:31
  5.6 8.3 %fusion.3 = f32[2,2,64,16,256]{4,3,2,1,0:T(8,128)S(1)} fusion(f32[2,2,64,16,256]{4,3,2,1,0:T(8,128)} %convert_element_type.64, f32[16]{0:T(128)S(1)} %get-tuple-element.133, f32[16]{0:T(128)S(1)} %get-tuple-element.134, f32[16]{0:T(128)S(1)} %get-tuple-element.135, f32[16]{0:T(128)S(1)} %get-tuple-element.132), kind=kLoop, calls=%fused_computation.14 | loop fusion | flops 7340032 | bytes 8388864 | tf_op jit(solution)/shard_map/add | solution.py:39
  14.0 2.0 fusion.120
  15.9 2.0 fusion.118
  17.9 2.0 fusion.119
  19.9 2.5 %add_convert_fusion = bf16[2,64,256,16]{2,3,1,0:T(8,128)(2,1)S(1)} fusion(f32[2,64,256,16]{2,3,1,0:T(8,128)S(1)} %fusion.120, f32[2,64,256,16]{2,3,1,0:T(8,128)S(1)} %fusion.118, f32[2,64,256,16]{2,3,1,0:T(8,128)S(1)} %fusion.119, f32[2,2,64,16,256]{4,3,2,1,0:T(8,128)S(1)} %fusion.3, f32[16]{0:T(128)S(1)} %iota_multiply_fusion), kind=kOutput, calls=%fused_computation.139 | convolution fusion | flops 103809536 | bytes 9437696 | tf_op jit(solution)/shard_map/km,bcmt->bckt/dot_general | solution.py:47
  22.4 2.1 copy.269
  24.5 7.4 %all-to-all-start = ((bf16[2,1024,256]{2,0,1:T(2,128)(2,1)}), bf16[2,1024,256]{2,0,1:T(2,128)(2,1)S(1)}, u32[]{:S(2)}, u32[]{:S(2)}) async-start(bf16[2,1024,256]{2,0,1:T(2,128)(2,1)} %copy.269), calls=%async_computation | async-start | bytes 2097152 | tf_op jit(solution)/shard_map/all_to_all | solution.py:91
  32.3 6.6 %broadcast_compare_fusion.31 = (pred[256,1024]{0,1:T(8,128)(4,1)S(1)}, pred[256,1024]{0,1:T(8,128)(4,1)S(1)}, pred[256,1024]{0,1:T(8,128)(4,1)S(1)}, pred[256,10...) fusion(s32[256,1024]{0,1:T(8,128)S(1)} %copy.274), kind=kLoop, calls=%fused_computation.254 | loop fusion | flops 8388608 | bytes 9437184 | tf_op jit(solution)/shard_map/eq | solution.py:100
  57.0 1.1 copy.309
  67.9 1.1 copy.283
  70.1 12.5 %copy.270 = bf16[2,1024,256]{1,2,0:T(8,128)(2,1)S(1)} copy(bf16[2,1024,256]{2,0,1:T(2,128)(2,1)S(1)} %all-to-all-done) | data formatting | bytes 2097152 | tf_op jit(solution)/shard_map/all_to_all | solution.py:91
  83.6 1.9 slice_bitcast_fusion.20
  85.5 2.0 slice_bitcast_fusion.29
  87.4 2.0 slice_bitcast_fusion.38
  89.5 2.1 fusion.122
  91.6 1.3 fusion.125
  93.0 1.3 fusion.128
  94.4 1.3 fusion.131
  95.8 1.3 fusion.134
  97.2 1.3 fusion.137
  98.6 1.3 fusion.140
  100.0 1.4 fusion.167
  101.9 1.5 collective-permute-done
  103.9 1.2 gather_fusion
  105.2 1.6 gather_fusion.1
  106.9 1.4 pad_select_fusion.19
  108.2 1.4 pad_select_fusion.18
  109.6 1.4 pad_select_fusion.17
  111.0 1.4 pad_select_fusion.16
  112.3 1.4 pad_select_fusion.15
  113.7 1.4 bitcast_add_fusion.3
  115.1 1.9 collective-permute-start.1
  117.1 12.3 %collective-permute-done.1 = f32[2,256,256]{2,0,1:T(2,128)S(1)} collective-permute-done((f32[2,256,256]{2,0,1:T(2,128)S(1)}, f32[2,256,256]{2,0,1:T(2,128)S(1)}, u32[]{:S(2)}, u32[]{:S(2)}) %collective-permute-start.1) | collective-permute-done | bytes 524320 | tf_op jit(solution)/shard_map/ppermute | solution.py:18
  129.4 1.2 gather_fusion.2
  130.7 1.2 gather_fusion.3
  131.9 1.4 pad_select_fusion.14
  133.3 1.4 pad_select_fusion.13
  134.7 1.4 pad_select_fusion.12
  136.0 1.4 pad_select_fusion.11
  137.4 1.4 pad_select_fusion.10
  138.8 1.6 bitcast_add_fusion.2
  140.3 1.7 collective-permute-start.2
  142.1 11.6 %collective-permute-done.2 = f32[2,256,256]{2,0,1:T(2,128)S(1)} collective-permute-done((f32[2,256,256]{2,0,1:T(2,128)S(1)}, f32[2,256,256]{2,0,1:T(2,128)S(1)}, u32[]{:S(2)}, u32[]{:S(2)}) %collective-permute-start.2) | collective-permute-done | bytes 524320 | tf_op jit(solution)/shard_map/ppermute | solution.py:18
  153.8 1.2 gather_fusion.4
  155.1 1.2 gather_fusion.5
  156.3 1.4 pad_select_fusion.9
  157.7 1.4 pad_select_fusion.8
  159.1 1.4 pad_select_fusion.7
  160.5 1.4 pad_select_fusion.6
  161.8 1.4 pad_select_fusion.5
  163.2 1.4 bitcast_add_fusion.1
  164.6 2.4 %collective-permute-start.3 = (f32[2,256,256]{2,0,1:T(2,128)S(1)}, f32[2,256,256]{2,0,1:T(2,128)S(1)}, u32[]{:S(2)}, u32[]{:S(2)}) collective-permute-start(f32[2,256,256]{2,0,1:T(2,128)S(1)} %bitcast_add_fusion.1), channel_id=1, source_target_pairs={{0,16},{2,18},{4,20},{6,22},{8,24},{10,26},{12,28},{14,30},{16,0},... | collective-permute-start | bytes 1572872 | tf_op jit(solution)/shard_map/ppermute | solution.py:18
  167.1 22.2 %collective-permute-done.3 = f32[2,256,256]{2,0,1:T(2,128)S(1)} collective-permute-done((f32[2,256,256]{2,0,1:T(2,128)S(1)}, f32[2,256,256]{2,0,1:T(2,128)S(1)}, u32[]{:S(2)}, u32[]{:S(2)}) %collective-permute-start.3) | collective-permute-done | bytes 524320 | tf_op jit(solution)/shard_map/ppermute | solution.py:18
  189.3 1.2 gather_fusion.7
  190.6 1.4 pad_select_fusion.4
  191.9 1.4 pad_select_fusion.3
  193.3 1.4 pad_select_fusion.2
  194.7 1.4 pad_select_fusion.1
  196.1 1.4 pad_select_fusion
  197.4 1.2 gather_fusion.6
  198.7 2.3 %fusion.268 = (f32[2,256]{0,1:T(8,128)S(1)}, f32[2,256,256]{2,0,1:T(2,128)S(1)}) fusion(f32[2,256,256]{2,0,1:T(2,128)S(1)} %pad_select_fusion, f32[2,256,224]{2,0,1:T(2,128)S(1)} %bitcast.432, pred[256]{0:T(512)(128)(4,1)S(1)} %get-tuple-element.21, f32[256,2,256]{2,1,0:T(2,128)S(1)} %gather_fusion.6), kind=kLoop, calls=%fused_computation.546 | loop fusion | flops 392704 | bytes 2033920 | tf_op jit(solution)/shard_map/reduce_sum | solution.py:70
  201.7 1.2 fusion.267
  209.1 1.3 add_reduce_fusion
  (183 shorter events, 40.0 us)
Async XLA Ops:
  22.4 9.5 %copy-start = (s32[256,1024]{1,0:T(8,128)S(1)}, s32[256,1024]{1,0:T(8,128)}, u32[]{:S(2)}) copy-start(s32[256,1024]{1,0:T(8,128)} %param.4) | copy-start | bytes 3145732
  24.5 45.6 %all-to-all-start = ((bf16[2,1024,256]{2,0,1:T(2,128)(2,1)}), bf16[2,1024,256]{2,0,1:T(2,128)(2,1)S(1)}, u32[]{:S(2)}, u32[]{:S(2)}) async-start(bf16[2,1024,256]{2,0,1:T(2,128)(2,1)} %copy.269), calls=%async_computation | async-start | bytes 2097152 | tf_op jit(solution)/shard_map/all_to_all | solution.py:91
  61.4 8.7 %copy-start.28 = (s32[4,3,256]{2,0,1:T(4,128)S(1)}, s32[4,3,256]{2,0,1:T(4,128)}, u32[]{:S(2)}) copy-start(s32[4,3,256]{2,0,1:T(4,128)} %param.5) | copy-start | bytes 36868
  89.5 2.1 %copy-start.1 = (pred[256,1,1024]{2,0,1:T(32,128)(4,1)S(1)}, pred[256,1,1024]{2,0,1:T(32,128)(4,1)}, u32[]{:S(2)}) copy-start(pred[256,1,1024]{2,0,1:T(32,128)(4,1)} %copy.356) | copy-start | bytes 786436
  89.5 2.1 %copy-start.2 = (pred[256,1,1024]{2,0,1:T(32,128)(4,1)S(1)}, pred[256,1,1024]{2,0,1:T(32,128)(4,1)}, u32[]{:S(2)}) copy-start(pred[256,1,1024]{2,0,1:T(32,128)(4,1)} %copy.355) | copy-start | bytes 786436
  89.5 2.1 copy-start.4
  91.6 1.4 copy-start.3
  91.6 1.4 copy-start.5
  91.6 1.4 copy-start.6
  91.6 1.4 copy-start.8
  93.0 1.4 copy-start.7
  93.0 1.4 copy-start.9
  93.0 1.4 copy-start.10
  93.0 1.4 copy-start.12
  94.4 1.4 copy-start.11
  94.4 1.4 copy-start.13
  94.4 1.4 copy-start.14
  94.4 1.4 copy-start.16
  95.8 1.4 copy-start.15
  95.8 1.4 copy-start.17
  95.8 1.4 copy-start.18
  95.8 1.4 copy-start.20
  97.2 1.4 copy-start.19
  97.2 1.4 copy-start.21
  97.2 1.4 copy-start.22
  97.2 1.4 copy-start.24
  98.6 1.4 copy-start.23
  98.6 1.4 copy-start.25
  98.6 1.4 copy-start.26
  98.6 1.4 copy-start.27
  98.6 1.4 copy-start.29
  101.4 2.0 collective-permute-start
  115.1 14.2 %collective-permute-start.1 = (f32[2,256,256]{2,0,1:T(2,128)S(1)}, f32[2,256,256]{2,0,1:T(2,128)S(1)}, u32[]{:S(2)}, u32[]{:S(2)}) collective-permute-start(f32[2,256,256]{2,0,1:T(2,128)S(1)} %bitcast_add_fusion.3), channel_id=1, source_target_pairs={{0,4},{2,6},{4,0},{6,2},{8,12},{10,14},{12,8},{14,10},{16,20},{18,... | collective-permute-start | bytes 1572872 | tf_op jit(solution)/shard_map/ppermute | solution.py:18
  140.3 13.4 %collective-permute-start.2 = (f32[2,256,256]{2,0,1:T(2,128)S(1)}, f32[2,256,256]{2,0,1:T(2,128)S(1)}, u32[]{:S(2)}, u32[]{:S(2)}) collective-permute-start(f32[2,256,256]{2,0,1:T(2,128)S(1)} %bitcast_add_fusion.2), channel_id=1, source_target_pairs={{0,8},{2,10},{4,12},{6,14},{8,0},{10,2},{12,4},{14,6},{16,24},{18,... | collective-permute-start | bytes 1572872 | tf_op jit(solution)/shard_map/ppermute | solution.py:18
  164.6 24.7 %collective-permute-start.3 = (f32[2,256,256]{2,0,1:T(2,128)S(1)}, f32[2,256,256]{2,0,1:T(2,128)S(1)}, u32[]{:S(2)}, u32[]{:S(2)}) collective-permute-start(f32[2,256,256]{2,0,1:T(2,128)S(1)} %bitcast_add_fusion.1), channel_id=1, source_target_pairs={{0,16},{2,18},{4,20},{6,22},{8,24},{10,26},{12,28},{14,30},{16,0},... | collective-permute-start | bytes 1572872 | tf_op jit(solution)/shard_map/ppermute | solution.py:18
where the time goes:
time: 215 us; the launch traced here: 212 us
  local copies, waits for them, and re-layouts  64.9 us (30%)
  other arithmetic  63.1 us (29%)
  waiting for transfers between devices  47.6 us (22%)
  matrix products  19.7 us (9%)
  starting transfers between devices  13.8 us (6%)
  between operations  2.34 us (1%)
    ppermute x4, waiting for transfers between devices, from_partner(): lax.ppermute(x, axis, [(i, i ^ 1 << distance) for i in range(lax.axis_siz...  47.6 us
    eq x64, local copies, waits for them, and re-layouts, local(): delay_table == first_shift + offset  31 us
    select_n x20, other arithmetic, delay_rows(): result = jnp.where(chosen, moved, result)  27.3 us
    all_to_all x1, local copies, waits for them, and re-layouts, local(): lax.all_to_all(filter_power(voltages), 'freq', split_axis=1, concat_axis=...  12.5 us
    dot_general x8, matrix products, local(): jnp.einsum('rsc,bsct->brt', onehot, shifted_block, preferred_element_type...  11.3 us
    add x1, other arithmetic, filter_power(): filtered + window[offset][:, None] * padded[..., TAPS - 1 - offset:TAPS -...  8.33 us
    all_to_all x1, starting transfers between devices, local(): lax.all_to_all(filter_power(voltages), 'freq', split_axis=1, concat_axis=...  7.36 us
    another operation x4, local copies, waits for them, and re-layouts, local(): jnp.stack([padded[:, :, SHIFTS - 1 - first_shift - offset:SHIFTS - 1 - fi...  6.75 us
  transfers between devices with their start and end apart: 5, of which 4 were waited for; matrix products, arithmetic and copies ran while one was open for 18% of the time, Pallas kernels for 0%

commit v1 on v0

v1 whole, which is shorter than its diff:
```python
import functools
import math

import jax
import jax.numpy as jnp
import ml_dtypes
import numpy as np
from jax import lax
from jax.experimental import pallas as pl
from jax.experimental.pallas import tpu as pltpu
from jax.sharding import PartitionSpec as P

TAPS = 4
WIDTHS = 8
SHIFTS = 32
CROSS_SHIFT = 64
PIECES = 3
VMEM_BYTES = 48 * 1024 * 1024
MESH = pl.DeviceIdType.MESH

epsilon = 1e-06


def filter_matrix(upchan):
    length = TAPS * upchan
    positions = np.arange(length, dtype=np.float64)
    window = np.sinc((positions - (length - 1) / 2.0) / upchan)
    window = window * (0.5 - 0.5 * np.cos(2.0 * math.pi * (positions + 0.5) / length))
    window = (window / np.sqrt(2.0 * np.sum(window * window))).reshape(TAPS, upchan)
    phase = np.arange(upchan)
    angle = 2.0 * math.pi * (phase[:, None] * phase[None, :] % upchan) / upchan
    cosine, sine = np.cos(angle), np.sin(angle)
    dft = np.stack([np.stack([cosine, sine], 1), np.stack([-sine, cosine], 1)], 0)
    full = dft[:, :, :, None, :] * window[None, None, None]
    full = full.reshape(2 * upchan, 2 * TAPS * upchan)
    pair = np.zeros((2, 2 * upchan, 2, 2 * TAPS * upchan))
    for channel in range(2):
        pair[channel, :, channel] = full
    pair = pair.reshape(4 * upchan, 4 * TAPS * upchan)
    rest, pieces = pair, []
    for _ in range(PIECES):
        piece = rest.astype(np.float32).astype(ml_dtypes.bfloat16)
        pieces.append(piece)
        rest = rest - piece.astype(np.float64)
    return np.concatenate(pieces, 0)


def filter_kernel(x_ref, w_ref, out_ref):
    _, beams, channels, upchan, samples = x_ref.shape
    width = beams * samples
    time = lax.broadcasted_iota(jnp.int32, (upchan, width), 1) % samples
    for first in range(0, channels, 2):
        tiles = []
        for channel in (first, first + 1):
            for part in range(2):
                signal = jnp.concatenate(
                    [x_ref[part, beam, channel] for beam in range(beams)], axis=1
                )
                tiles.append(signal)
                signal = signal.astype(jnp.float32)
                for tap in range(1, TAPS):
                    moved = jnp.where(time >= tap, pltpu.roll(signal, tap, 1), 0.0)
                    tiles.append(moved.astype(jnp.bfloat16))
        stacked = jnp.concatenate(tiles, axis=0)
        spectrum = jnp.dot(w_ref[...], stacked, preferred_element_type=jnp.float32)
        rows = 4 * upchan
        total = spectrum[2 * rows :] + spectrum[rows : 2 * rows]
        total = total + spectrum[:rows]
        for offset in range(2):
            real = total[2 * offset * upchan : (2 * offset + 1) * upchan]
            imag = total[(2 * offset + 1) * upchan : (2 * offset + 2) * upchan]
            start = (first + offset) * upchan
            out_ref[start : start + upchan, :] = (real * real + imag * imag).astype(jnp.bfloat16)


def filter_power(volts):
    _, beams, channels, upchan, samples = volts.shape
    block = min(8, channels)
    weights = jnp.asarray(filter_matrix(upchan))
    return pl.pallas_call(
        filter_kernel,
        grid=(channels // block,),
        in_specs=[
            pl.BlockSpec((2, beams, block, upchan, samples), lambda i: (0, 0, i, 0, 0)),
            pl.BlockSpec(weights.shape, lambda i: (0, 0)),
        ],
        out_specs=pl.BlockSpec((block * upchan, beams * samples), lambda i: (i, 0)),
        out_shape=jax.ShapeDtypeStruct((channels * upchan, beams * samples), jnp.bfloat16),
        compiler_params=pltpu.CompilerParams(vmem_limit_bytes=VMEM_BYTES),
        name="filterbank",
    )(volts, weights)


def dedisperse_kernel(sources, upchan, samples, x_ref, delay_ref, out_ref, ordered, total):
    channels, width = x_ref.shape
    each = channels // (sources * upchan)
    for source in range(sources):
        for index in range(each):
            start = (source * each + index) * upchan
            goal = (index * sources + source) * upchan
            ordered[goal : goal + upchan, :] = x_ref[start : start + upchan, :]
    total[...] = jnp.zeros_like(total)
    inside = lax.broadcasted_iota(jnp.int32, total.shape, 1) % samples >= 1

    def step(count, carry):
        shift = SHIFTS - 1 - count
        onehot = jnp.where(delay_ref[...] == shift, 1.0, 0.0).astype(jnp.bfloat16)
        term = jnp.dot(onehot, ordered[...], preferred_element_type=jnp.float32)
        total[...] = jnp.where(inside, pltpu.roll(total[...], 1, 1), 0.0) + term
        return carry

    lax.fori_loop(0, SHIFTS, step, 0)
    for beam in range(width // samples):
        out_ref[beam] = total[:, beam * samples : (beam + 1) * samples].T


def dedisperse(intensity, delays, sources, upchan, samples):
    rows = delays.shape[0]
    channels, width = intensity.shape
    return pl.pallas_call(
        functools.partial(dedisperse_kernel, sources, upchan, samples),
        out_shape=jax.ShapeDtypeStruct((width // samples, samples, rows), jnp.float32),
        in_specs=[pl.BlockSpec(memory_space=pltpu.VMEM)] * 2,
        out_specs=pl.BlockSpec(memory_space=pltpu.VMEM),
        scratch_shapes=[
            pltpu.VMEM((channels, width), jnp.bfloat16),
            pltpu.VMEM((rows, width), jnp.float32),
        ],
        compiler_params=pltpu.CompilerParams(vmem_limit_bytes=VMEM_BYTES),
        name="dedisperse",
    )(intensity, delays)


def later(series, amount):
    if amount % 8 == 0:
        zeros = jnp.zeros((amount, series.shape[1]), series.dtype)
        return jnp.concatenate([zeros, series[:-amount]], axis=0)
    time = lax.broadcasted_iota(jnp.int32, series.shape, 0)
    return jnp.where(time >= amount, pltpu.roll(series, amount, 0), 0.0)


def permuted(series, index):
    samples, rows = series.shape
    chosen = lax.broadcasted_iota(jnp.int32, (rows, index.shape[1]), 0) == index
    chosen = jnp.where(chosen, 1.0, 0.0).astype(jnp.bfloat16)
    rest, pieces = series, []
    for _ in range(PIECES):
        piece = rest.astype(jnp.bfloat16)
        pieces.append(piece)
        rest = rest - piece.astype(jnp.float32)
    moved = jnp.dot(
        jnp.concatenate(pieces, axis=0), chosen, preferred_element_type=jnp.float32
    )
    return (moved[:samples] + moved[samples : 2 * samples]) + moved[2 * samples :]


def merge_kernel(n, z_ref, table_ref, out_ref, pair, state, peaks, landed, sems, end_send, end_recv):
    levels = n.bit_length() - 1
    me = lax.axis_index("freq")
    half = n // 2
    barrier = pltpu.get_barrier_semaphore()
    partners = [me + (1 - 2 * (me // 2**level % 2)) * 2**level for level in range(levels)]
    goals = [slot * half + me // 2 for slot in range(2)]
    origins = [2 * (me % half) + beam for beam in range(2)]
    for partner in partners:
        pl.semaphore_signal(barrier, inc=1, device_id={"freq": partner}, device_id_type=MESH)
    for origin in origins:

        @pl.when(origin != me)
        def _():
            pl.semaphore_signal(barrier, inc=1, device_id={"freq": origin}, device_id_type=MESH)

    pl.semaphore_wait(barrier, levels + 1 + (me + n - 1) // n - (me + 1) // n)

    bit_count = max(CROSS_SHIFT - 1, 1).bit_length()
    final = None
    for level in range(levels):
        bit = me // 2**level % 2
        held = z_ref if level == 0 else state.at[level - 1]
        copy = pltpu.make_async_remote_copy(
            src_ref=held.at[1 - bit],
            dst_ref=pair.at[level, bit],
            send_sem=sems.at[0, level],
            recv_sem=sems.at[1, level],
            device_id={"freq": partners[level]},
            device_id_type=MESH,
        )
        copy.start()
        pair[level, bit] = held[bit]
        base = me // 2 ** (level + 1) * 2 ** (level + 1) + me // 2 % 2**level
        tables = [table_ref[base + slot * 2**level, level] for slot in range(2)]
        lower_index, upper_index, delays = (
            jnp.concatenate([table[row : row + 1] for table in tables], axis=1)
            for row in range(3)
        )
        copy.wait()
        upper = permuted(pair[level, 1], upper_index)
        for count in range(bit_count):
            upper = jnp.where((delays >> count) & 1 == 1, later(upper, 2**count), upper)
        merged = permuted(pair[level, 0], lower_index) + upper
        if level < levels - 1:
            rows = merged.shape[1] // 2
            state[level, 0] = merged[:, :rows]
            state[level, 1] = merged[:, rows:]
        else:
            final = merged

    samples, width = final.shape
    centred = final - jnp.mean(final, axis=0, keepdims=True)
    boxcar = centred * lax.rsqrt(jnp.mean(centred * centred, axis=0, keepdims=True) + epsilon)
    maxima = [jnp.max(boxcar, axis=0, keepdims=True)]
    for count in range(1, WIDTHS):
        boxcar = boxcar + later(boxcar, 2 ** (count - 1))
        maxima.append(jnp.max(boxcar, axis=0, keepdims=True) / math.sqrt(2**count))
    maxima = jnp.concatenate(maxima, axis=0)
    rows = width // 2
    beam = me % 2

    def send(slot):
        return pltpu.make_async_remote_copy(
            src_ref=peaks.at[slot],
            dst_ref=landed.at[beam],
            send_sem=end_send.at[slot],
            recv_sem=end_recv.at[beam],
            device_id={"freq": goals[slot]},
            device_id_type=MESH,
        )

    for slot in range(2):
        peaks[slot] = maxima[:, slot * rows : (slot + 1) * rows]
    for slot in range(2):

        @pl.when(goals[slot] != me)
        def _():
            send(slot).start()

        @pl.when(goals[slot] == me)
        def _():
            landed[beam] = peaks[slot]

    for slot in range(2):

        @pl.when(goals[slot] != me)
        def _():
            send(slot).wait_send()

    for source in range(2):

        @pl.when(origins[source] != me)
        def _():
            pltpu.make_async_remote_copy(
                src_ref=peaks.at[0],
                dst_ref=landed.at[source],
                send_sem=end_send.at[0],
                recv_sem=end_recv.at[source],
                device_id={"freq": origins[source]},
                device_id_type=MESH,
            ).wait_recv()

    out_ref[...] = landed[...]


def merge(series, tables, n):
    beams, samples, rows = series.shape
    levels = n.bit_length() - 1
    return pl.pallas_call(
        functools.partial(merge_kernel, n),
        out_shape=jax.ShapeDtypeStruct((beams, WIDTHS, rows), jnp.float32),
        in_specs=[pl.BlockSpec(memory_space=pltpu.VMEM)] * 2,
        out_specs=pl.BlockSpec(memory_space=pltpu.VMEM),
        scratch_shapes=[
            pltpu.VMEM((levels, 2, samples, rows), jnp.float32),
            pltpu.VMEM((levels - 1, 2, samples, rows), jnp.float32),
            pltpu.VMEM((2, WIDTHS, rows), jnp.float32),
            pltpu.VMEM((2, WIDTHS, rows), jnp.float32),
            pltpu.SemaphoreType.DMA((2, levels)),
            pltpu.SemaphoreType.DMA((2,)),
            pltpu.SemaphoreType.DMA((2,)),
        ],
        compiler_params=pltpu.CompilerParams(
            collective_id=1, has_side_effects=True, vmem_limit_bytes=VMEM_BYTES
        ),
        name="merge",
    )(series, tables)


def local(voltages, sub_delays, merge_tables):
    n = lax.axis_size("freq")
    upchan, samples = voltages.shape[3:]
    tables = lax.all_gather(merge_tables, "freq", axis=0)
    intensity = lax.all_to_all(
        filter_power(voltages), "freq", split_axis=0, concat_axis=0, tiled=True
    )
    series = dedisperse(intensity, sub_delays, n, upchan, samples)
    return merge(series, tables, n)


def solution(mesh):
    return jax.shard_map(
        local,
        mesh=mesh,
        in_specs=(P(None, "beam", "freq", None, None), P("freq", None), P(None, None, "freq")),
        out_specs=P("beam", None, "freq"),
        check_vma=False,
    )
```

time: 215 us -> 104 us (0.48)
  the two profiles are of different devices: /device:TPU:0 before, /device:TPU:1 now
where the time goes in v1:
time: 104 us; the launch traced here: 103 us
  Pallas kernels  58.5 us (56%)
  blocking collectives  34.4 us (33%)
  starting transfers between devices  7.32 us (7%)
  local copies, waits for them, and re-layouts  3.1 us (3%)
    pallas_call x1, Pallas kernels, merge(): pl.pallas_call(functools.partial(merge_kernel, n), out_shape=jax.ShapeDty...  38.7 us
    all_gather x1, blocking collectives, local(): tables = lax.all_gather(merge_tables, 'freq', axis=0)  34.4 us
    pallas_call x1, Pallas kernels, dedisperse(): pl.pallas_call(functools.partial(dedisperse_kernel, sources, upchan, samp...  14.7 us
    all_to_all x1, starting transfers between devices, local(): lax.all_to_all(filter_power(voltages), 'freq', split_axis=0, concat_axis=...  7.32 us
    pallas_call x1, Pallas kernels, filter_power(): pl.pallas_call(filter_kernel, grid=(channels // block,), in_specs=[pl.Blo...  5.06 us
    unnamed x10, local copies, waits for them, and re-layouts  3.1 us
  transfers between devices with their start and end apart: 1, of which 0 were waited for; matrix products, arithmetic and copies ran while one was open for 0% of the time, Pallas kernels for 0%

profile of v1, /device:TPU:1, one launch (start us, length us, event | category | flops | bytes accessed | tf_op | source)
XLA Modules:
  0.0 103.3 jit_solution(14603979143893111699)
XLA Ops:
  0.0 0.0 copy-start
  0.0 1.6 %copy-done = bf16[2,2,64,16,256]{4,3,2,1,0:T(8,128)(2,1)S(1)} copy-done((bf16[2,2,64,16,256]{4,3,2,1,0:T(8,128)(2,1)S(1)}, bf16[2,2,64,16,256]{4,3,2,1,0:T(8,128)(2,1)}, u32[]{:S(2)}) %copy-start) | copy-done | bytes 2097176
  1.6 0.0 copy-start.2
  1.6 0.9 copy-done.2
  2.5 0.0 copy-start.3
  2.5 0.0 copy-start.1
  2.5 5.1 %filterbank.1 = bf16[1024,512]{1,0:T(8,128)(2,1)} custom-call(bf16[2,2,64,16,256]{4,3,2,1,0:T(8,128)(2,1)S(1)} %copy-done, bf16[192,256]{1,0:T(8,128)(2,1)S(1)} %copy-done.2), custom_call_target="tpu_custom_call" | custom-call | tf_op jit(solution)/shard_map/filterbank/pallas_call | solution.py:80
  7.6 7.3 %all-to-all-start = ((bf16[16,64,512]{2,1,0:T(8,128)(2,1)}), bf16[16,64,512]{2,1,0:T(8,128)(2,1)S(1)}, u32[]{:S(2)}, u32[]{:S(2)}) async-start(bf16[16,64,512]{2,1,0:T(8,128)(2,1)} %bitcast), calls=%async_computation | async-start | bytes 2097152 | tf_op jit(solution)/shard_map/all_to_all | solution.py:291
  14.9 0.0 copy-done.3
  14.9 34.4 %all-gather = s32[64,3,256]{2,1,0:T(4,128)S(1)} all-gather(s32[4,3,256]{2,1,0:T(4,128)S(1)} %copy.6), channel_id=2, replica_groups=mesh['freq'=16,'beam'=2] {'freq'}, dimensions={0}, use_global_device_ids=true | all-gather | bytes 208896 | tf_op jit(solution)/shard_map/all_gather | solution.py:290
  49.3 0.0 all-to-all-done
  49.3 0.0 copy-done.1
  49.3 14.7 %dedisperse.1.z_ref = f32[2,256,256]{2,1,0:T(8,128)S(1)} custom-call(bf16[1024,512]{1,0:T(8,128)(2,1)S(1)} %bitcast.3, s32[256,1024]{1,0:T(8,128)S(1)} %copy-done.1), custom_call_target="tpu_custom_call" | custom-call | tf_op jit(solution)/shard_map/dedisperse/pallas_call | solution.py:120
  64.0 38.7 %merge.1 = f32[2,8,256]{2,1,0:T(8,128)S(1)} custom-call(f32[2,256,256]{2,1,0:T(8,128)S(1)} %dedisperse.1.z_ref, s32[16,4,3,256]{3,2,1,0:T(4,128)S(1)} %bitcast.4), custom_call_target="tpu_custom_call" | custom-call | tf_op jit(solution)/shard_map/merge/pallas_call | solution.py:266
  102.7 0.6 copy.8
  (1 shorter events, 0.0 us)
Async XLA Ops:
  0.0 1.6 %copy-start = (bf16[2,2,64,16,256]{4,3,2,1,0:T(8,128)(2,1)S(1)}, bf16[2,2,64,16,256]{4,3,2,1,0:T(8,128)(2,1)}, u32[]{:S(2)}) copy-start(bf16[2,2,64,16,256]{4,3,2,1,0:T(8,128)(2,1)} %x_ref.1) | copy-start | bytes 6291460
  1.6 0.9 copy-start.2
  2.5 12.4 %copy-start.3 = (s32[4,3,256]{2,0,1:T(4,128)S(1)}, s32[4,3,256]{2,0,1:T(4,128)}, u32[]{:S(2)}) copy-start(s32[4,3,256]{2,0,1:T(4,128)} %param.6) | copy-start | bytes 36868
  2.5 46.8 %copy-start.1 = (s32[256,1024]{1,0:T(8,128)S(1)}, s32[256,1024]{1,0:T(8,128)}, u32[]{:S(2)}) copy-start(s32[256,1024]{1,0:T(8,128)} %delay_ref.1) | copy-start | bytes 3145732
  7.6 41.7 %all-to-all-start = ((bf16[16,64,512]{2,1,0:T(8,128)(2,1)}), bf16[16,64,512]{2,1,0:T(8,128)(2,1)S(1)}, u32[]{:S(2)}, u32[]{:S(2)}) async-start(bf16[16,64,512]{2,1,0:T(8,128)(2,1)} %bitcast), calls=%async_computation | async-start | bytes 2097152 | tf_op jit(solution)/shard_map/all_to_all | solution.py:291

commit v2 on v1

--- a/solution.py
+++ b/solution.py
@@ -13,6 +13,7 @@
 TAPS = 4
 WIDTHS = 8
 SHIFTS = 32
+STRIDE = 4
 CROSS_SHIFT = 64
 PIECES = 3
 VMEM_BYTES = 48 * 1024 * 1024
@@ -21,7 +22,7 @@
 epsilon = 1e-06
 
 
-def filter_matrix(upchan):
+def filter_matrix(upchan, count):
     length = TAPS * upchan
     positions = np.arange(length, dtype=np.float64)
     window = np.sinc((positions - (length - 1) / 2.0) / upchan)
@@ -33,10 +34,10 @@
     dft = np.stack([np.stack([cosine, sine], 1), np.stack([-sine, cosine], 1)], 0)
     full = dft[:, :, :, None, :] * window[None, None, None]
     full = full.reshape(2 * upchan, 2 * TAPS * upchan)
-    pair = np.zeros((2, 2 * upchan, 2, 2 * TAPS * upchan))
-    for channel in range(2):
+    pair = np.zeros((count, 2 * upchan, count, 2 * TAPS * upchan))
+    for channel in range(count):
         pair[channel, :, channel] = full
-    pair = pair.reshape(4 * upchan, 4 * TAPS * upchan)
+    pair = pair.reshape(2 * count * upchan, 2 * count * TAPS * upchan)
     rest, pieces = pair, []
     for _ in range(PIECES):
         piece = rest.astype(np.float32).astype(ml_dtypes.bfloat16)
@@ -45,16 +46,17 @@
     return np.concatenate(pieces, 0)
 
 
-def filter_kernel(x_ref, w_ref, out_ref):
-    _, beams, channels, upchan, samples = x_ref.shape
+def filter_chunk(x_ref, w_ref, first_channel, channels, write):
+    _, beams, _, upchan, samples = x_ref.shape
     width = beams * samples
+    count = w_ref.shape[1] // (2 * TAPS * upchan)
     time = lax.broadcasted_iota(jnp.int32, (upchan, width), 1) % samples
-    for first in range(0, channels, 2):
+    for first in range(0, channels, count):
         tiles = []
-        for channel in (first, first + 1):
+        for channel in range(first, first + count):
             for part in range(2):
                 signal = jnp.concatenate(
-                    [x_ref[part, beam, channel] for beam in range(beams)], axis=1
+                    [x_ref[part, beam, first_channel + channel] for beam in range(beams)], axis=1
                 )
                 tiles.append(signal)
                 signal = signal.astype(jnp.float32)
@@ -63,72 +65,240 @@
                     tiles.append(moved.astype(jnp.bfloat16))
         stacked = jnp.concatenate(tiles, axis=0)
         spectrum = jnp.dot(w_ref[...], stacked, preferred_element_type=jnp.float32)
-        rows = 4 * upchan
+        rows = 2 * count * upchan
         total = spectrum[2 * rows :] + spectrum[rows : 2 * rows]
         total = total + spectrum[:rows]
-        for offset in range(2):
+        for offset in range(count):
             real = total[2 * offset * upchan : (2 * offset + 1) * upchan]
             imag = total[(2 * offset + 1) * upchan : (2 * offset + 2) * upchan]
-            start = (first + offset) * upchan
-            out_ref[start : start + upchan, :] = (real * real + imag * imag).astype(jnp.bfloat16)
-
-
-def filter_power(volts):
-    _, beams, channels, upchan, samples = volts.shape
-    block = min(8, channels)
-    weights = jnp.asarray(filter_matrix(upchan))
+            write(first + offset, (real * real + imag * imag).astype(jnp.bfloat16))
+
+
+def exclusive_or(me, other, n):
+    result = 0
+    for bit in range(n.bit_length() - 1):
+        result = result + (me // 2**bit % 2 + other // 2**bit % 2) % 2 * 2**bit
+    return result
+
+
+def table_places(me, level):
+    size = 2**level
+    base = me // (2 * size) * (2 * size)
+    goals = [base + me % size * 2 + beam for beam in range(2)]
+    origins = [base + me // 2 % size + slot * size for slot in range(2)]
+    return goals, origins
+
+
+def subband_kernel(
+    n,
+    x_ref,
+    w_ref,
+    delay_ref,
+    table_ref,
+    out_ref,
+    tables_ref,
+    outgoing,
+    arrived,
+    local_delays,
+    shifted,
+    total,
+    part,
+    tables,
+    send_sem,
+    recv_sem,
+    table_send,
+    table_recv,
+):
+    levels = n.bit_length() - 1
+    me = lax.axis_index("freq")
+    samples = x_ref.shape[4]
+    _, each, upchan, width = arrived.shape
+    rows, channels = delay_ref.shape
+    groups, _, depth = local_delays.shape
+    members = n // groups
+
+    barrier = pltpu.get_barrier_semaphore()
+
+    def greet(offset, carry):
+        pl.semaphore_signal(
+            barrier, inc=1, device_id={"freq": (me + offset) % n}, device_id_type=MESH
+        )
+        return carry
+
+    lax.fori_loop(1, n, greet, 0)
+    pl.semaphore_wait(barrier, n - 1)
+
+    def table_copy(level, beam):
+        goals, _ = table_places(me, level)
+        slot = me // 2**level % 2
+        return goals[beam], pltpu.make_async_remote_copy(
+            src_ref=table_ref.at[level],
+            dst_ref=tables.at[level, slot],
+            send_sem=table_send.at[level, beam],
+            recv_sem=table_recv.at[level, slot],
+            device_id={"freq": goals[beam]},
+            device_id_type=MESH,
+        )
+
+    def table_arrival(level, slot):
+        _, origins = table_places(me, level)
+        return origins[slot], pltpu.make_async_remote_copy(
+            src_ref=table_ref.at[level],
+            dst_ref=tables.at[level, slot],
+            send_sem=table_send.at[level, 0],
+            recv_sem=table_recv.at[level, slot],
+            device_id={"freq": origins[slot]},
+            device_id_type=MESH,
+        )
+
+    def chunk_copy(offset):
+        return pltpu.make_async_remote_copy(
+            src_ref=outgoing.at[offset],
+            dst_ref=arrived.at[offset],
+            send_sem=send_sem.at[offset],
+            recv_sem=recv_sem.at[offset],
+            device_id={"freq": exclusive_or(me, offset, n)},
+            device_id_type=MESH,
+        )
+
+    def send_chunk(step, carry):
+        offset = n - 1 - step
+
+        def write(index, tile):
+            outgoing[offset, index] = tile
+
+        filter_chunk(x_ref, w_ref, exclusive_or(me, offset, n) * each, each, write)
+        chunk_copy(offset).start()
+        return carry
+
+    lax.fori_loop(0, n - 1, send_chunk, 0)
+
+    def write_own(index, tile):
+        arrived[0, index] = tile
+
+    filter_chunk(x_ref, w_ref, me * each, each, write_own)
+
+    for level in range(levels):
+        for beam in range(2):
+            goal, copy = table_copy(level, beam)
+
+            @pl.when(goal != me)
+            def _():
+                copy.start()
+
+            @pl.when(goal == me)
+            def _():
+                tables[level, me // 2**level % 2] = table_ref[level]
+
+    delays = delay_ref[...].astype(jnp.float32).astype(jnp.bfloat16)
+    for group in range(groups):
+        column = lax.broadcasted_iota(jnp.int32, (channels, depth), 1)
+        index, fine = column // upchan % each, column % upchan
+        source = me ^ (group * members + column // (each * upchan))
+        wanted = index * (n * upchan) + source * upchan + fine
+        chosen = lax.broadcasted_iota(jnp.int32, (channels, depth), 0) == wanted
+        chosen = jnp.where(chosen, 1.0, 0.0).astype(jnp.bfloat16)
+        local_delays[group] = jnp.dot(
+            delays, chosen, preferred_element_type=jnp.float32
+        ).astype(jnp.int32)
+
+    time = lax.broadcasted_iota(jnp.int32, (depth, width), 1) % samples
+    inside = lax.broadcasted_iota(jnp.int32, (rows, width), 1) % samples >= STRIDE
+    for group in range(groups):
+        for offset in range(group * members, (group + 1) * members):
+            if offset > 0:
+                chunk_copy(offset).wait_recv()
+        block = arrived[group * members : (group + 1) * members].reshape(depth, width)
+        shifted[:depth] = block
+        block = block.astype(jnp.float32)
+        for shift in range(1, STRIDE):
+            moved = jnp.where(time >= shift, pltpu.roll(block, shift, 1), 0.0)
+            shifted[shift * depth : (shift + 1) * depth] = moved.astype(jnp.bfloat16)
+        part[...] = jnp.zeros_like(part)
+
+        def horner(step, carry):
+            base = SHIFTS - STRIDE - STRIDE * step
+            group_delays = local_delays[group]
+            onehot = jnp.concatenate(
+                [
+                    jnp.where(group_delays == base + shift, 1.0, 0.0).astype(jnp.bfloat16)
+                    for shift in range(STRIDE)
+                ],
+                axis=1,
+            )
+            term = jnp.dot(onehot, shifted[...], preferred_element_type=jnp.float32)
+            part[...] = jnp.where(inside, pltpu.roll(part[...], STRIDE, 1), 0.0) + term
+            return carry
+
+        lax.fori_loop(0, SHIFTS // STRIDE, horner, 0)
+        if group == 0:
+            total[...] = part[...]
+        elif group < groups - 1:
+            total[...] += part[...]
+    summed = total[...] + part[...] if groups > 1 else part[...]
+    for beam in range(width // samples):
+        out_ref[beam] = summed[:, beam * samples : (beam + 1) * samples].T
+
+    for level in range(levels):
+        for slot in range(2):
+            origin, arrival = table_arrival(level, slot)
+
+            @pl.when(origin != me)
+            def _():
+                arrival.wait_recv()
+
+        for beam in range(2):
+            goal, copy = table_copy(level, beam)
+
+            @pl.when(goal != me)
+            def _():
+                copy.wait_send()
+
+    tables_ref[...] = tables[...]
+
+    def sent(offset, carry):
+        chunk_copy(offset).wait_send()
+        return carry
+
+    lax.fori_loop(1, n, sent, 0)
+
+
+def subbands(volts, delays, merge_tables, n):
+    _, beams, coarse, upchan, samples = volts.shape
+    rows, channels = delays.shape
+    levels = n.bit_length() - 1
+    each = coarse // n
+    width = beams * samples
+    members = max(1, min(n, 256 // (each * upchan)))
+    depth = members * each * upchan
+    weights = jnp.asarray(filter_matrix(upchan, 2 if each % 2 == 0 else 1))
+    vmem = pl.BlockSpec(memory_space=pltpu.VMEM)
     return pl.pallas_call(
-        filter_kernel,
-        grid=(channels // block,),
-        in_specs=[
-            pl.BlockSpec((2, beams, block, upchan, samples), lambda i: (0, 0, i, 0, 0)),
-            pl.BlockSpec(weights.shape, lambda i: (0, 0)),
+        functools.partial(subband_kernel, n),
+        out_shape=(
+            jax.ShapeDtypeStruct((beams, samples, rows), jnp.float32),
+            jax.ShapeDtypeStruct((levels, 2, 3, rows), jnp.int32),
+        ),
+        in_specs=[vmem] * 4,
+        out_specs=(vmem, vmem),
+        scratch_shapes=[
+            pltpu.VMEM((n, each, upchan, width), jnp.bfloat16),
+            pltpu.VMEM((n, each, upchan, width), jnp.bfloat16),
+            pltpu.VMEM((n // members, rows, depth), jnp.int32),
+            pltpu.VMEM((STRIDE * depth, width), jnp.bfloat16),
+            pltpu.VMEM((rows, width), jnp.float32),
+            pltpu.VMEM((rows, width), jnp.float32),
+            pltpu.VMEM((levels, 2, 3, rows), jnp.int32),
+            pltpu.SemaphoreType.DMA((n,)),
+            pltpu.SemaphoreType.DMA((n,)),
+            pltpu.SemaphoreType.DMA((levels, 2)),
+            pltpu.SemaphoreType.DMA((levels, 2)),
         ],
-        out_specs=pl.BlockSpec((block * upchan, beams * samples), lambda i: (i, 0)),
-        out_shape=jax.ShapeDtypeStruct((channels * upchan, beams * samples), jnp.bfloat16),
-        compiler_params=pltpu.CompilerParams(vmem_limit_bytes=VMEM_BYTES),
-        name="filterbank",
-    )(volts, weights)
-
-
-def dedisperse_kernel(sources, upchan, samples, x_ref, delay_ref, out_ref, ordered, total):
-    channels, width = x_ref.shape
-    each = channels // (sources * upchan)
-    for source in range(sources):
-        for index in range(each):
-            start = (source * each + index) * upchan
-            goal = (index * sources + source) * upchan
-            ordered[goal : goal + upchan, :] = x_ref[start : start + upchan, :]
-    total[...] = jnp.zeros_like(total)
-    inside = lax.broadcasted_iota(jnp.int32, total.shape, 1) % samples >= 1
-
-    def step(count, carry):
-        shift = SHIFTS - 1 - count
-        onehot = jnp.where(delay_ref[...] == shift, 1.0, 0.0).astype(jnp.bfloat16)
-        term = jnp.dot(onehot, ordered[...], preferred_element_type=jnp.float32)
-        total[...] = jnp.where(inside, pltpu.roll(total[...], 1, 1), 0.0) + term
-        return carry
-
-    lax.fori_loop(0, SHIFTS, step, 0)
-    for beam in range(width // samples):
-        out_ref[beam] = total[:, beam * samples : (beam + 1) * samples].T
-
-
-def dedisperse(intensity, delays, sources, upchan, samples):
-    rows = delays.shape[0]
-    channels, width = intensity.shape
-    return pl.pallas_call(
-        functools.partial(dedisperse_kernel, sources, upchan, samples),
-        out_shape=jax.ShapeDtypeStruct((width // samples, samples, rows), jnp.float32),
-        in_specs=[pl.BlockSpec(memory_space=pltpu.VMEM)] * 2,
-        out_specs=pl.BlockSpec(memory_space=pltpu.VMEM),
-        scratch_shapes=[
-            pltpu.VMEM((channels, width), jnp.bfloat16),
-            pltpu.VMEM((rows, width), jnp.float32),
-        ],
-        compiler_params=pltpu.CompilerParams(vmem_limit_bytes=VMEM_BYTES),
-        name="dedisperse",
-    )(intensity, delays)
+        compiler_params=pltpu.CompilerParams(
+            collective_id=0, has_side_effects=True, vmem_limit_bytes=VMEM_BYTES
+        ),
+        name="subbands",
+    )(volts, weights, delays, merge_tables)
 
 
 def later(series, amount):
@@ -187,8 +357,7 @@
         )
         copy.start()
         pair[level, bit] = held[bit]
-        base = me // 2 ** (level + 1) * 2 ** (level + 1) + me // 2 % 2**level
-        tables = [table_ref[base + slot * 2**level, level] for slot in range(2)]
+        tables = [table_ref[level, slot] for slot in range(2)]
         lower_index, upper_index, delays = (
             jnp.concatenate([table[row : row + 1] for table in tables], axis=1)
             for row in range(3)
@@ -286,12 +455,7 @@
 
 def local(voltages, sub_delays, merge_tables):
     n = lax.axis_size("freq")
-    upchan, samples = voltages.shape[3:]
-    tables = lax.all_gather(merge_tables, "freq", axis=0)
-    intensity = lax.all_to_all(
-        filter_power(voltages), "freq", split_axis=0, concat_axis=0, tiled=True
-    )
-    series = dedisperse(intensity, sub_delays, n, upchan, samples)
+    series, tables = subbands(voltages, sub_delays, merge_tables, n)
     return merge(series, tables, n)
 
 

time: 104 us -> 81.4 us (0.78)
  blocking collectives: 34.4 us -> 0 us
  Pallas kernels: 58.5 us -> 76.1 us
  starting transfers between devices: 7.32 us -> 0 us
  local copies, waits for them, and re-layouts: 3.1 us -> 5.03 us
    all_gather x1 -> x0, blocking collectives: 34.4 us -> none  [local(): tables = lax.all_gather(merge_tables, 'freq', axis=0)]
    pallas_call x2 -> x1, Pallas kernels: 19.8 us -> 39.6 us  [subbands(): pl.pallas_call(functools.partial(subband_kernel, n), out_shape=(jax.Shape...]
    all_to_all x1 -> x0, starting transfers between devices: 7.32 us -> none  [local(): lax.all_to_all(filter_power(voltages), 'freq', split_axis=0, concat_axis=...]
    pallas_call x1, Pallas kernels: 38.7 us -> 36.4 us  [merge(): pl.pallas_call(functools.partial(merge_kernel, n), out_shape=jax.ShapeDty...]
    unnamed x10 -> x8, local copies, waits for them, and re-layouts: 3.1 us -> 5.03 us
  transfers between devices with their start and end apart: 1 -> 0, of which waited for: 0 -> 0; matrix products, arithmetic and copies ran while one was open for 0% -> 0% of each run, Pallas kernels for 0% -> 0%
where the time goes in v2:
time: 81.4 us; the launch traced here: 81.1 us
  Pallas kernels  76.1 us (93%)
  local copies, waits for them, and re-layouts  5.03 us (6%)
    pallas_call x1, Pallas kernels, subbands(): pl.pallas_call(functools.partial(subband_kernel, n), out_shape=(jax.Shape...  39.6 us
    pallas_call x1, Pallas kernels, merge(): pl.pallas_call(functools.partial(merge_kernel, n), out_shape=jax.ShapeDty...  36.4 us
    unnamed x8, local copies, waits for them, and re-layouts  5.03 us

profile of v2, /device:TPU:1, one launch (start us, length us, event | category | flops | bytes accessed | tf_op | source)
XLA Modules:
  0.0 81.1 jit_solution(14337781092116727645)
XLA Ops:
  0.0 0.7 copy.5.table_ref
  0.7 0.0 copy-start
  0.7 1.6 %copy-done = bf16[2,2,64,16,256]{4,3,2,1,0:T(8,128)(2,1)S(1)} copy-done((bf16[2,2,64,16,256]{4,3,2,1,0:T(8,128)(2,1)S(1)}, bf16[2,2,64,16,256]{4,3,2,1,0:T(8,128)(2,1)}, u32[]{:S(2)}) %copy-start) | copy-done | bytes 2097176
  2.3 0.0 copy-start.1
  2.3 1.2 %copy-done.1 = s32[256,1024]{1,0:T(8,128)S(1)} copy-done((s32[256,1024]{1,0:T(8,128)S(1)}, s32[256,1024]{1,0:T(8,128)}, u32[]{:S(2)}) %copy-start.1) | copy-done | bytes 1048600
  3.5 0.0 copy-start.2
  3.5 0.9 %copy-done.2 = bf16[192,256]{1,0:T(8,128)(2,1)S(1)} copy-done((bf16[192,256]{1,0:T(8,128)(2,1)S(1)}, bf16[192,256]{1,0:T(8,128)(2,1)}, u32[]{:S(2)}) %copy-start.2) | copy-done | bytes 98328
  4.4 39.6 %subbands.1 = (f32[2,256,256]{2,1,0:T(8,128)S(1)}, s32[4,2,3,256]{3,2,1,0:T(4,128)S(1)}) custom-call(bf16[2,2,64,16,256]{4,3,2,1,0:T(8,128)(2,1)S(1)} %copy-done, bf16[192,256]{1,0:T(8,128)(2,1)S(1)} %copy-done.2, s32[256,1024]{1,0:T(8,128)S(1)} %copy-done.1, s32[4,3,256]{2,1,0:T(4,128)S(1)} %copy.5.table_ref), custom_call_target="tpu_custom_call" | custom-call | tf_op jit(solution)/shard_map/subbands/pallas_call | solution.py:276
  44.1 36.4 %merge.1 = f32[2,8,256]{2,1,0:T(8,128)S(1)} custom-call(f32[2,256,256]{2,1,0:T(8,128)S(1)} %get-tuple-element.7.z_ref, s32[4,2,3,256]{3,2,1,0:T(4,128)S(1)} %get-tuple-element.8.table_ref), custom_call_target="tpu_custom_call" | custom-call | tf_op jit(solution)/shard_map/merge/pallas_call | solution.py:435
  80.5 0.6 copy.7
Async XLA Ops:
  0.7 1.6 %copy-start = (bf16[2,2,64,16,256]{4,3,2,1,0:T(8,128)(2,1)S(1)}, bf16[2,2,64,16,256]{4,3,2,1,0:T(8,128)(2,1)}, u32[]{:S(2)}) copy-start(bf16[2,2,64,16,256]{4,3,2,1,0:T(8,128)(2,1)} %x_ref.1) | copy-start | bytes 6291460
  2.3 1.2 %copy-start.1 = (s32[256,1024]{1,0:T(8,128)S(1)}, s32[256,1024]{1,0:T(8,128)}, u32[]{:S(2)}) copy-start(s32[256,1024]{1,0:T(8,128)} %delay_ref.1) | copy-start | bytes 3145732
  3.5 0.9 %copy-start.2 = (bf16[192,256]{1,0:T(8,128)(2,1)S(1)}, bf16[192,256]{1,0:T(8,128)(2,1)}, u32[]{:S(2)}) copy-start(bf16[192,256]{1,0:T(8,128)(2,1)} %constant.2.clone.w_ref) | copy-start | bytes 294916

commit v3 on v2

--- a/solution.py
+++ b/solution.py
@@ -17,6 +17,7 @@
 CROSS_SHIFT = 64
 PIECES = 3
 VMEM_BYTES = 48 * 1024 * 1024
+SUBBAND_BYTES = 63 * 1024 * 1024
 MESH = pl.DeviceIdType.MESH
 
 epsilon = 1e-06
@@ -91,12 +92,18 @@
 
 def subband_kernel(
     n,
+    x_hbm,
+    w_hbm,
+    delay_hbm,
+    table_hbm,
+    out_ref,
+    tables_ref,
     x_ref,
     w_ref,
     delay_ref,
     table_ref,
-    out_ref,
-    tables_ref,
+    weights,
+    level_tables,
     outgoing,
     arrived,
     local_delays,
@@ -108,6 +115,7 @@
     recv_sem,
     table_send,
     table_recv,
+    input_sem,
 ):
     levels = n.bit_length() - 1
     me = lax.axis_index("freq")
@@ -117,6 +125,15 @@
     groups, _, depth = local_delays.shape
     members = n // groups
 
+    inputs = [
+        pltpu.make_async_copy(source, goal, input_sem.at[place])
+        for place, (source, goal) in enumerate(
+            [(x_hbm, x_ref), (w_hbm, w_ref), (delay_hbm, delay_ref), (table_hbm, table_ref)]
+        )
+    ]
+    for copy in inputs:
+        copy.start()
+
     barrier = pltpu.get_barrier_semaphore()
 
     def greet(offset, carry):
@@ -127,12 +144,15 @@
 
     lax.fori_loop(1, n, greet, 0)
     pl.semaphore_wait(barrier, n - 1)
+    inputs[0].wait()
+    inputs[1].wait()
+    weights[...] = w_ref[...].astype(jnp.bfloat16)
 
     def table_copy(level, beam):
         goals, _ = table_places(me, level)
         slot = me // 2**level % 2
         return goals[beam], pltpu.make_async_remote_copy(
-            src_ref=table_ref.at[level],
+            src_ref=level_tables.at[level],
             dst_ref=tables.at[level, slot],
             send_sem=table_send.at[level, beam],
             recv_sem=table_recv.at[level, slot],
@@ -143,7 +163,7 @@
     def table_arrival(level, slot):
         _, origins = table_places(me, level)
         return origins[slot], pltpu.make_async_remote_copy(
-            src_ref=table_ref.at[level],
+            src_ref=level_tables.at[level],
             dst_ref=tables.at[level, slot],
             send_sem=table_send.at[level, 0],
             recv_sem=table_recv.at[level, slot],
@@ -161,22 +181,30 @@
             device_id_type=MESH,
         )
 
-    def send_chunk(step, carry):
-        offset = n - 1 - step
+    def send_chunk(offset, carry):
 
         def write(index, tile):
             outgoing[offset, index] = tile
 
-        filter_chunk(x_ref, w_ref, exclusive_or(me, offset, n) * each, each, write)
+        filter_chunk(x_ref, weights, exclusive_or(me, offset, n) * each, each, write)
         chunk_copy(offset).start()
         return carry
 
-    lax.fori_loop(0, n - 1, send_chunk, 0)
+    half = n // 2
+    early = min(half + members, n)
+    lax.fori_loop(half, early, send_chunk, 0)
+    lax.fori_loop(1, half, send_chunk, 0)
 
     def write_own(index, tile):
         arrived[0, index] = tile
 
-    filter_chunk(x_ref, w_ref, me * each, each, write_own)
+    filter_chunk(x_ref, weights, me * each, each, write_own)
+    lax.fori_loop(early, n, send_chunk, 0)
+    inputs[2].wait()
+    inputs[3].wait()
+    for level in range(levels):
+        for row in range(3):
+            level_tables[level, row : row + 1] = table_ref[row, level : level + 1]
 
     for level in range(levels):
         for beam in range(2):
@@ -188,11 +216,11 @@
 
             @pl.when(goal == me)
             def _():
-                tables[level, me // 2**level % 2] = table_ref[level]
+                tables[level, me // 2**level % 2] = level_tables[level]
 
     delays = delay_ref[...].astype(jnp.float32).astype(jnp.bfloat16)
     for group in range(groups):
-        column = lax.broadcasted_iota(jnp.int32, (channels, depth), 1)
+        column = lax.broadcasted_iota(jnp.int32, (1, depth), 1)
         index, fine = column // upchan % each, column % upchan
         source = me ^ (group * members + column // (each * upchan))
         wanted = index * (n * upchan) + source * upchan + fine
@@ -271,7 +299,8 @@
     width = beams * samples
     members = max(1, min(n, 256 // (each * upchan)))
     depth = members * each * upchan
-    weights = jnp.asarray(filter_matrix(upchan, 2 if each % 2 == 0 else 1))
+    weights = jnp.asarray(filter_matrix(upchan, 2 if each % 2 == 0 else 1).astype(np.float32))
+    merge_tables = merge_tables.transpose(1, 0, 2)
     vmem = pl.BlockSpec(memory_space=pltpu.VMEM)
     return pl.pallas_call(
         functools.partial(subband_kernel, n),
@@ -279,9 +308,15 @@
             jax.ShapeDtypeStruct((beams, samples, rows), jnp.float32),
             jax.ShapeDtypeStruct((levels, 2, 3, rows), jnp.int32),
         ),
-        in_specs=[vmem] * 4,
+        in_specs=[pl.BlockSpec(memory_space=pltpu.HBM)] * 4,
         out_specs=(vmem, vmem),
         scratch_shapes=[
+            pltpu.VMEM(volts.shape, volts.dtype),
+            pltpu.VMEM(weights.shape, weights.dtype),
+            pltpu.VMEM(delays.shape, delays.dtype),
+            pltpu.VMEM(merge_tables.shape, merge_tables.dtype),
+            pltpu.VMEM(weights.shape, jnp.bfloat16),
+            pltpu.VMEM((levels, 3, rows), jnp.int32),
             pltpu.VMEM((n, each, upchan, width), jnp.bfloat16),
             pltpu.VMEM((n, each, upchan, width), jnp.bfloat16),
             pltpu.VMEM((n // members, rows, depth), jnp.int32),
@@ -293,9 +328,10 @@
             pltpu.SemaphoreType.DMA((n,)),
             pltpu.SemaphoreType.DMA((levels, 2)),
             pltpu.SemaphoreType.DMA((levels, 2)),
+            pltpu.SemaphoreType.DMA((4,)),
         ],
         compiler_params=pltpu.CompilerParams(
-            collective_id=0, has_side_effects=True, vmem_limit_bytes=VMEM_BYTES
+            collective_id=0, has_side_effects=True, vmem_limit_bytes=SUBBAND_BYTES
         ),
         name="subbands",
     )(volts, weights, delays, merge_tables)
@@ -309,10 +345,24 @@
     return jnp.where(time >= amount, pltpu.roll(series, amount, 0), 0.0)
 
 
-def permuted(series, index):
-    samples, rows = series.shape
-    chosen = lax.broadcasted_iota(jnp.int32, (rows, index.shape[1]), 0) == index
-    chosen = jnp.where(chosen, 1.0, 0.0).astype(jnp.bfloat16)
+def delayed(before, series, delays):
+    count = series.shape[0]
+    current = jnp.concatenate([before, series], axis=0)
+    for bit in reversed(range(max(CROSS_SHIFT - 1, 1).bit_length())):
+        amount = 2**bit
+        chosen = (delays >> bit) & 1 == 1
+        if amount >= 8:
+            height = count + -(-(amount - 1) // 8) * 8
+            first = current.shape[0] - height
+            moved = current[first - amount : first - amount + height]
+            current = jnp.where(chosen, moved, current[first:])
+        else:
+            current = jnp.where(chosen, pltpu.roll(current, amount, 0), current)
+    return current[current.shape[0] - count :]
+
+
+def permuted(series, chosen):
+    samples = series.shape[0]
     rest, pieces = series, []
     for _ in range(PIECES):
         piece = rest.astype(jnp.bfloat16)
@@ -324,7 +374,9 @@
     return (moved[:samples] + moved[samples : 2 * samples]) + moved[2 * samples :]
 
 
-def merge_kernel(n, z_ref, table_ref, out_ref, pair, state, peaks, landed, sems, end_send, end_recv):
+def merge_kernel(
+    n, z_ref, table_ref, out_ref, taken, state, chosen, previous, final, peaks, landed, sems, end_send, end_recv
+):
     levels = n.bit_length() - 1
     me = lax.axis_index("freq")
     half = n // 2
@@ -342,39 +394,57 @@
 
     pl.semaphore_wait(barrier, levels + 1 + (me + n - 1) // n - (me + 1) // n)
 
-    bit_count = max(CROSS_SHIFT - 1, 1).bit_length()
-    final = None
-    for level in range(levels):
-        bit = me // 2**level % 2
+    samples, width = final.shape
+    rows = width // 2
+    piece = min(CROSS_SHIFT, samples)
+    chunks = samples // piece
+
+    def exchange(level, chunk):
         held = z_ref if level == 0 else state.at[level - 1]
-        copy = pltpu.make_async_remote_copy(
-            src_ref=held.at[1 - bit],
-            dst_ref=pair.at[level, bit],
-            send_sem=sems.at[0, level],
-            recv_sem=sems.at[1, level],
+        span = pl.ds(chunk * piece, piece)
+        return pltpu.make_async_remote_copy(
+            src_ref=held.at[1 - me // 2**level % 2, span],
+            dst_ref=taken.at[level, span],
+            send_sem=sems.at[0, level, chunk],
+            recv_sem=sems.at[1, level, chunk],
             device_id={"freq": partners[level]},
             device_id_type=MESH,
         )
-        copy.start()
-        pair[level, bit] = held[bit]
-        tables = [table_ref[level, slot] for slot in range(2)]
-        lower_index, upper_index, delays = (
-            jnp.concatenate([table[row : row + 1] for table in tables], axis=1)
-            for row in range(3)
-        )
-        copy.wait()
-        upper = permuted(pair[level, 1], upper_index)
-        for count in range(bit_count):
-            upper = jnp.where((delays >> count) & 1 == 1, later(upper, 2**count), upper)
-        merged = permuted(pair[level, 0], lower_index) + upper
-        if level < levels - 1:
-            rows = merged.shape[1] // 2
-            state[level, 0] = merged[:, :rows]
-            state[level, 1] = merged[:, rows:]
-        else:
-            final = merged
-
-    samples, width = final.shape
+
+    def columns(level, row):
+        return jnp.concatenate([table_ref[level, slot, row : row + 1] for slot in range(2)], axis=1)
+
+    for chunk in range(chunks):
+        exchange(0, chunk).start()
+    for level in range(levels):
+        for row in range(2):
+            onehot = lax.broadcasted_iota(jnp.int32, (rows, width), 0) == columns(level, row)
+            chosen[level, row] = jnp.where(onehot, 1.0, 0.0).astype(jnp.bfloat16)
+    for diagonal in range(levels + chunks - 1):
+        for level in reversed(range(levels)):
+            chunk = diagonal - level
+            if not 0 <= chunk < chunks:
+                continue
+            span = slice(chunk * piece, (chunk + 1) * piece)
+            bit = me // 2**level % 2
+            kept = z_ref[bit, span] if level == 0 else state[level - 1, bit, span]
+            exchange(level, chunk).wait_recv()
+            other = taken[level, span]
+            lower = jnp.where(bit == 0, kept, other)
+            upper = jnp.where(bit == 0, other, kept)
+            upper = permuted(upper, chosen[level, 1])
+            before = jnp.zeros_like(upper) if chunk == 0 else previous[level]
+            if chunk < chunks - 1:
+                previous[level] = upper
+            merged = permuted(lower, chosen[level, 0]) + delayed(before, upper, columns(level, 2))
+            if level < levels - 1:
+                state[level, 0, span] = merged[:, :rows]
+                state[level, 1, span] = merged[:, rows:]
+                exchange(level + 1, chunk).start()
+            else:
+                final[span] = merged
+
+    final = final[...]
     centred = final - jnp.mean(final, axis=0, keepdims=True)
     boxcar = centred * lax.rsqrt(jnp.mean(centred * centred, axis=0, keepdims=True) + epsilon)
     maxima = [jnp.max(boxcar, axis=0, keepdims=True)]
@@ -382,7 +452,6 @@
         boxcar = boxcar + later(boxcar, 2 ** (count - 1))
         maxima.append(jnp.max(boxcar, axis=0, keepdims=True) / math.sqrt(2**count))
     maxima = jnp.concatenate(maxima, axis=0)
-    rows = width // 2
     beam = me % 2
 
     def send(slot):
@@ -427,6 +496,9 @@
             ).wait_recv()
 
     out_ref[...] = landed[...]
+    for level in range(levels):
+        for chunk in range(chunks):
+            exchange(level, chunk).wait_send()
 
 
 def merge(series, tables, n):
@@ -438,11 +510,14 @@
         in_specs=[pl.BlockSpec(memory_space=pltpu.VMEM)] * 2,
         out_specs=pl.BlockSpec(memory_space=pltpu.VMEM),
         scratch_shapes=[
-            pltpu.VMEM((levels, 2, samples, rows), jnp.float32),
+            pltpu.VMEM((levels, samples, rows), jnp.float32),
             pltpu.VMEM((levels - 1, 2, samples, rows), jnp.float32),
+            pltpu.VMEM((levels, 2, rows, 2 * rows), jnp.bfloat16),
+            pltpu.VMEM((levels, min(CROSS_SHIFT, samples), 2 * rows), jnp.float32),
+            pltpu.VMEM((samples, 2 * rows), jnp.float32),
             pltpu.VMEM((2, WIDTHS, rows), jnp.float32),
             pltpu.VMEM((2, WIDTHS, rows), jnp.float32),
-            pltpu.SemaphoreType.DMA((2, levels)),
+            pltpu.SemaphoreType.DMA((2, levels, samples // min(CROSS_SHIFT, samples))),
             pltpu.SemaphoreType.DMA((2,)),
             pltpu.SemaphoreType.DMA((2,)),
         ],

time: 81.4 us -> 76.9 us (0.945)
  local copies, waits for them, and re-layouts: 5.03 us -> 2.4 us
  Pallas kernels: 76.1 us -> 74.3 us
    unnamed x8 -> x5, local copies, waits for them, and re-layouts: 5.03 us -> 2.4 us
    pallas_call x1, Pallas kernels: 36.4 us -> 34.2 us  [merge(): pl.pallas_call(functools.partial(merge_kernel, n), out_shape=jax.ShapeDty...]
where the time goes in v3:
time: 76.9 us; the launch traced here: 76.7 us
  Pallas kernels  74.3 us (97%)
  local copies, waits for them, and re-layouts  2.4 us (3%)
    pallas_call x1, Pallas kernels, subbands(): pl.pallas_call(functools.partial(subband_kernel, n), out_shape=(jax.Shape...  40.1 us
    pallas_call x1, Pallas kernels, merge(): pl.pallas_call(functools.partial(merge_kernel, n), out_shape=jax.ShapeDty...  34.2 us
    unnamed x5, local copies, waits for them, and re-layouts  2.4 us

profile of v3, /device:TPU:1, one launch (start us, length us, event | category | flops | bytes accessed | tf_op | source)
XLA Modules:
  0.0 76.7 jit_solution(1980125335821450902)
XLA Ops:
  0.0 40.1 %subbands.1 = (f32[2,256,256]{2,1,0:T(8,128)}, s32[4,2,3,256]{3,2,1,0:T(4,128)}) custom-call(bf16[2,2,64,16,256]{4,3,2,1,0:T(8,128)(2,1)} %x_hbm.1, f32[192,256]{1,0:T(8,128)} %constant.2.clone.w_hbm, s32[256,1024]{1,0:T(8,128)} %delay_hbm.1, s32[3,4,256]{2,1,0:T(4,128)} %bitcast.1), custom_call_target="tpu_custom_call" | custom-call | tf_op jit(solution)/shard_map/subbands/pallas_call | solution.py:305
  40.1 0.0 copy-start
  40.1 1.0 %copy-done = f32[2,256,256]{2,1,0:T(8,128)S(1)} copy-done((f32[2,256,256]{2,1,0:T(8,128)S(1)}, f32[2,256,256]{2,1,0:T(8,128)}, u32[]{:S(2)}) %copy-start) | copy-done | bytes 524312
  41.2 0.0 copy-start.1
  41.2 0.8 copy-done.1
  41.9 34.2 %merge.1 = f32[2,8,256]{2,1,0:T(8,128)S(1)} custom-call(f32[2,256,256]{2,1,0:T(8,128)S(1)} %copy-done, s32[4,2,3,256]{3,2,1,0:T(4,128)S(1)} %copy-done.1), custom_call_target="tpu_custom_call" | custom-call | tf_op jit(solution)/shard_map/merge/pallas_call | solution.py:507
  76.1 0.6 copy.6
Async XLA Ops:
  40.1 1.0 %copy-start = (f32[2,256,256]{2,1,0:T(8,128)S(1)}, f32[2,256,256]{2,1,0:T(8,128)}, u32[]{:S(2)}) copy-start(f32[2,256,256]{2,1,0:T(8,128)} %get-tuple-element.7.z_ref) | copy-start | bytes 1572868
  41.2 0.8 copy-start.1

commit v4 on v3

--- a/solution.py
+++ b/solution.py
@@ -13,11 +13,11 @@
 TAPS = 4
 WIDTHS = 8
 SHIFTS = 32
+LANES = 128
 STRIDE = 4
 CROSS_SHIFT = 64
 PIECES = 3
-VMEM_BYTES = 48 * 1024 * 1024
-SUBBAND_BYTES = 63 * 1024 * 1024
+VMEM_BYTES = 63 * 1024 * 1024
 MESH = pl.DeviceIdType.MESH
 
 epsilon = 1e-06
@@ -97,7 +97,6 @@
     delay_hbm,
     table_hbm,
     out_ref,
-    tables_ref,
     x_ref,
     w_ref,
     delay_ref,
@@ -116,6 +115,8 @@
     table_send,
     table_recv,
     input_sem,
+    series,
+    *merge_scratch,
 ):
     levels = n.bit_length() - 1
     me = lax.axis_index("freq")
@@ -265,7 +266,7 @@
             total[...] += part[...]
     summed = total[...] + part[...] if groups > 1 else part[...]
     for beam in range(width // samples):
-        out_ref[beam] = summed[:, beam * samples : (beam + 1) * samples].T
+        series[beam] = summed[:, beam * samples : (beam + 1) * samples].T
 
     for level in range(levels):
         for slot in range(2):
@@ -282,7 +283,7 @@
             def _():
                 copy.wait_send()
 
-    tables_ref[...] = tables[...]
+    merge_series(n, series, tables, out_ref, *merge_scratch)
 
     def sent(offset, carry):
         chunk_copy(offset).wait_send()
@@ -297,19 +298,16 @@
     levels = n.bit_length() - 1
     each = coarse // n
     width = beams * samples
+    piece = min(CROSS_SHIFT, samples)
     members = max(1, min(n, 256 // (each * upchan)))
     depth = members * each * upchan
     weights = jnp.asarray(filter_matrix(upchan, 2 if each % 2 == 0 else 1).astype(np.float32))
     merge_tables = merge_tables.transpose(1, 0, 2)
-    vmem = pl.BlockSpec(memory_space=pltpu.VMEM)
     return pl.pallas_call(
         functools.partial(subband_kernel, n),
-        out_shape=(
-            jax.ShapeDtypeStruct((beams, samples, rows), jnp.float32),
-            jax.ShapeDtypeStruct((levels, 2, 3, rows), jnp.int32),
-        ),
+        out_shape=jax.ShapeDtypeStruct((beams, WIDTHS, rows), jnp.float32),
         in_specs=[pl.BlockSpec(memory_space=pltpu.HBM)] * 4,
-        out_specs=(vmem, vmem),
+        out_specs=pl.BlockSpec(memory_space=pltpu.VMEM),
         scratch_shapes=[
             pltpu.VMEM(volts.shape, volts.dtype),
             pltpu.VMEM(weights.shape, weights.dtype),
@@ -329,9 +327,19 @@
             pltpu.SemaphoreType.DMA((levels, 2)),
             pltpu.SemaphoreType.DMA((levels, 2)),
             pltpu.SemaphoreType.DMA((4,)),
+            pltpu.VMEM((beams, samples, rows), jnp.float32),
+            pltpu.VMEM((levels, samples, rows), jnp.float32),
+            pltpu.VMEM((levels - 1, 2, samples, rows), jnp.float32),
+            pltpu.VMEM((levels, piece, 2 * rows), jnp.float32),
+            pltpu.VMEM((samples, 2 * rows), jnp.float32),
+            pltpu.VMEM((2, WIDTHS, rows), jnp.float32),
+            pltpu.VMEM((2, WIDTHS, rows), jnp.float32),
+            pltpu.SemaphoreType.DMA((2, levels, samples // piece)),
+            pltpu.SemaphoreType.DMA((2,)),
+            pltpu.SemaphoreType.DMA((2,)),
         ],
         compiler_params=pltpu.CompilerParams(
-            collective_id=0, has_side_effects=True, vmem_limit_bytes=SUBBAND_BYTES
+            collective_id=0, has_side_effects=True, vmem_limit_bytes=VMEM_BYTES
         ),
         name="subbands",
     )(volts, weights, delays, merge_tables)
@@ -361,39 +369,38 @@
     return current[current.shape[0] - count :]
 
 
-def permuted(series, chosen):
-    samples = series.shape[0]
-    rest, pieces = series, []
-    for _ in range(PIECES):
-        piece = rest.astype(jnp.bfloat16)
-        pieces.append(piece)
-        rest = rest - piece.astype(jnp.float32)
-    moved = jnp.dot(
-        jnp.concatenate(pieces, axis=0), chosen, preferred_element_type=jnp.float32
-    )
-    return (moved[:samples] + moved[samples : 2 * samples]) + moved[2 * samples :]
-
-
-def merge_kernel(
-    n, z_ref, table_ref, out_ref, taken, state, chosen, previous, final, peaks, landed, sems, end_send, end_recv
+def permuted(series, index):
+    samples, rows = series.shape
+    lanes = min(LANES, rows)
+    columns = []
+    for first in range(0, index.shape[1], lanes):
+        wanted = jnp.broadcast_to(index[:, first : first + lanes], (samples, lanes))
+        place = wanted & (lanes - 1)
+        result = None
+        for start in range(0, rows, lanes):
+            found = jnp.take_along_axis(
+                series[:, start : start + lanes], place, axis=1, mode="promise_in_bounds"
+            )
+            result = found if start == 0 else jnp.where(wanted >= start, found, result)
+        columns.append(result)
+    return jnp.concatenate(columns, axis=1)
+
+
+def merge_places(me, n):
+    half = n // 2
+    levels = n.bit_length() - 1
+    partners = [me + (1 - 2 * (me // 2**level % 2)) * 2**level for level in range(levels)]
+    goals = [slot * half + me // 2 for slot in range(2)]
+    origins = [2 * (me % half) + beam for beam in range(2)]
+    return partners, goals, origins
+
+
+def merge_series(
+    n, z_ref, table_ref, out_ref, taken, state, previous, final, peaks, landed, sems, end_send, end_recv
 ):
     levels = n.bit_length() - 1
     me = lax.axis_index("freq")
-    half = n // 2
-    barrier = pltpu.get_barrier_semaphore()
-    partners = [me + (1 - 2 * (me // 2**level % 2)) * 2**level for level in range(levels)]
-    goals = [slot * half + me // 2 for slot in range(2)]
-    origins = [2 * (me % half) + beam for beam in range(2)]
-    for partner in partners:
-        pl.semaphore_signal(barrier, inc=1, device_id={"freq": partner}, device_id_type=MESH)
-    for origin in origins:
-
-        @pl.when(origin != me)
-        def _():
-            pl.semaphore_signal(barrier, inc=1, device_id={"freq": origin}, device_id_type=MESH)
-
-    pl.semaphore_wait(barrier, levels + 1 + (me + n - 1) // n - (me + 1) // n)
-
+    partners, goals, origins = merge_places(me, n)
     samples, width = final.shape
     rows = width // 2
     piece = min(CROSS_SHIFT, samples)
@@ -416,10 +423,6 @@
 
     for chunk in range(chunks):
         exchange(0, chunk).start()
-    for level in range(levels):
-        for row in range(2):
-            onehot = lax.broadcasted_iota(jnp.int32, (rows, width), 0) == columns(level, row)
-            chosen[level, row] = jnp.where(onehot, 1.0, 0.0).astype(jnp.bfloat16)
     for diagonal in range(levels + chunks - 1):
         for level in reversed(range(levels)):
             chunk = diagonal - level
@@ -432,11 +435,11 @@
             other = taken[level, span]
             lower = jnp.where(bit == 0, kept, other)
             upper = jnp.where(bit == 0, other, kept)
-            upper = permuted(upper, chosen[level, 1])
+            upper = permuted(upper, columns(level, 1))
             before = jnp.zeros_like(upper) if chunk == 0 else previous[level]
             if chunk < chunks - 1:
                 previous[level] = upper
-            merged = permuted(lower, chosen[level, 0]) + delayed(before, upper, columns(level, 2))
+            merged = permuted(lower, columns(level, 0)) + delayed(before, upper, columns(level, 2))
             if level < levels - 1:
                 state[level, 0, span] = merged[:, :rows]
                 state[level, 1, span] = merged[:, rows:]
@@ -501,37 +504,9 @@
             exchange(level, chunk).wait_send()
 
 
-def merge(series, tables, n):
-    beams, samples, rows = series.shape
-    levels = n.bit_length() - 1
-    return pl.pallas_call(
-        functools.partial(merge_kernel, n),
-        out_shape=jax.ShapeDtypeStruct((beams, WIDTHS, rows), jnp.float32),
-        in_specs=[pl.BlockSpec(memory_space=pltpu.VMEM)] * 2,
-        out_specs=pl.BlockSpec(memory_space=pltpu.VMEM),
-        scratch_shapes=[
-            pltpu.VMEM((levels, samples, rows), jnp.float32),
-            pltpu.VMEM((levels - 1, 2, samples, rows), jnp.float32),
-            pltpu.VMEM((levels, 2, rows, 2 * rows), jnp.bfloat16),
-            pltpu.VMEM((levels, min(CROSS_SHIFT, samples), 2 * rows), jnp.float32),
-            pltpu.VMEM((samples, 2 * rows), jnp.float32),
-            pltpu.VMEM((2, WIDTHS, rows), jnp.float32),
-            pltpu.VMEM((2, WIDTHS, rows), jnp.float32),
-            pltpu.SemaphoreType.DMA((2, levels, samples // min(CROSS_SHIFT, samples))),
-            pltpu.SemaphoreType.DMA((2,)),
-            pltpu.SemaphoreType.DMA((2,)),
-        ],
-        compiler_params=pltpu.CompilerParams(
-            collective_id=1, has_side_effects=True, vmem_limit_bytes=VMEM_BYTES
-        ),
-        name="merge",
-    )(series, tables)
-
-
 def local(voltages, sub_delays, merge_tables):
     n = lax.axis_size("freq")
-    series, tables = subbands(voltages, sub_delays, merge_tables, n)
-    return merge(series, tables, n)
+    return subbands(voltages, sub_delays, merge_tables, n)
 
 
 def solution(mesh):

time: 76.9 us -> 73.5 us (0.956)
  Pallas kernels: 74.3 us -> 71.9 us
  local copies, waits for them, and re-layouts: 2.4 us -> 1.32 us
    pallas_call x2 -> x1, Pallas kernels: 74.3 us -> 71.9 us  [subbands(): pl.pallas_call(functools.partial(subband_kernel, n), out_shape=jax.ShapeD...]
    unnamed x5 -> x1, local copies, waits for them, and re-layouts: 2.4 us -> 1.32 us
where the time goes in v4:
time: 73.5 us; the launch traced here: 73.2 us
  Pallas kernels  71.9 us (98%)
  local copies, waits for them, and re-layouts  1.32 us (2%)
    pallas_call x1, Pallas kernels, subbands(): pl.pallas_call(functools.partial(subband_kernel, n), out_shape=jax.ShapeD...  71.9 us

profile of v4, /device:TPU:1, one launch (start us, length us, event | category | flops | bytes accessed | tf_op | source)
XLA Modules:
  0.0 73.2 jit_solution(10987937453928530507)
XLA Ops:
  0.0 71.9 %subbands.1 = f32[2,8,256]{2,1,0:T(8,128)} custom-call(bf16[2,2,64,16,256]{4,3,2,1,0:T(8,128)(2,1)} %x_hbm.1, f32[192,256]{1,0:T(8,128)} %constant.2.clone.w_hbm, s32[256,1024]{1,0:T(8,128)} %delay_hbm.1, s32[3,4,256]{2,1,0:T(4,128)} %bitcast.1), custom_call_target="tpu_custom_call" | custom-call | tf_op jit(solution)/shard_map/subbands/pallas_call | solution.py:306
  71.9 1.3 %copy.6 = f32[2,8,256]{2,1,0:T(8,128)} copy(f32[2,8,256]{2,1,0:T(8,128)} %subbands.1) | data formatting | bytes 32768

commit v5 on v4

--- a/solution.py
+++ b/solution.py
@@ -14,6 +14,7 @@
 WIDTHS = 8
 SHIFTS = 32
 LANES = 128
+PIECE = 32
 STRIDE = 4
 CROSS_SHIFT = 64
 PIECES = 3
@@ -298,7 +299,7 @@
     levels = n.bit_length() - 1
     each = coarse // n
     width = beams * samples
-    piece = min(CROSS_SHIFT, samples)
+    piece = min(PIECE, samples)
     members = max(1, min(n, 256 // (each * upchan)))
     depth = members * each * upchan
     weights = jnp.asarray(filter_matrix(upchan, 2 if each % 2 == 0 else 1).astype(np.float32))
@@ -330,7 +331,7 @@
             pltpu.VMEM((beams, samples, rows), jnp.float32),
             pltpu.VMEM((levels, samples, rows), jnp.float32),
             pltpu.VMEM((levels - 1, 2, samples, rows), jnp.float32),
-            pltpu.VMEM((levels, piece, 2 * rows), jnp.float32),
+            pltpu.VMEM((levels, CROSS_SHIFT, 2 * rows), jnp.float32),
             pltpu.VMEM((samples, 2 * rows), jnp.float32),
             pltpu.VMEM((2, WIDTHS, rows), jnp.float32),
             pltpu.VMEM((2, WIDTHS, rows), jnp.float32),
@@ -395,6 +396,19 @@
     return partners, goals, origins
 
 
+def chunk_order(levels, chunks):
+    expected = {}
+    for level in range(levels):
+        wire = 0.2 if level == 0 else 1.3 if level == levels - 1 else 0.65
+        delay = 0.5 if level == 0 else 1.0
+        free = 0.0
+        for chunk in range(chunks):
+            ready = expected[level - 1, chunk] + 0.25 if level else 0.0
+            free = max(free, ready) + wire
+            expected[level, chunk] = free + delay
+    return sorted(expected, key=lambda step: (expected[step], step))
+
+
 def merge_series(
     n, z_ref, table_ref, out_ref, taken, state, previous, final, peaks, landed, sems, end_send, end_recv
 ):
@@ -403,7 +417,7 @@
     partners, goals, origins = merge_places(me, n)
     samples, width = final.shape
     rows = width // 2
-    piece = min(CROSS_SHIFT, samples)
+    piece = min(PIECE, samples)
     chunks = samples // piece
 
     def exchange(level, chunk):
@@ -423,29 +437,25 @@
 
     for chunk in range(chunks):
         exchange(0, chunk).start()
-    for diagonal in range(levels + chunks - 1):
-        for level in reversed(range(levels)):
-            chunk = diagonal - level
-            if not 0 <= chunk < chunks:
-                continue
-            span = slice(chunk * piece, (chunk + 1) * piece)
-            bit = me // 2**level % 2
-            kept = z_ref[bit, span] if level == 0 else state[level - 1, bit, span]
-            exchange(level, chunk).wait_recv()
-            other = taken[level, span]
-            lower = jnp.where(bit == 0, kept, other)
-            upper = jnp.where(bit == 0, other, kept)
-            upper = permuted(upper, columns(level, 1))
-            before = jnp.zeros_like(upper) if chunk == 0 else previous[level]
-            if chunk < chunks - 1:
-                previous[level] = upper
-            merged = permuted(lower, columns(level, 0)) + delayed(before, upper, columns(level, 2))
-            if level < levels - 1:
-                state[level, 0, span] = merged[:, :rows]
-                state[level, 1, span] = merged[:, rows:]
-                exchange(level + 1, chunk).start()
-            else:
-                final[span] = merged
+    for level, chunk in chunk_order(levels, chunks):
+        span = slice(chunk * piece, (chunk + 1) * piece)
+        bit = me // 2**level % 2
+        kept = z_ref[bit, span] if level == 0 else state[level - 1, bit, span]
+        exchange(level, chunk).wait_recv()
+        other = taken[level, span]
+        lower = jnp.where(bit == 0, kept, other)
+        upper = jnp.where(bit == 0, other, kept)
+        upper = permuted(upper, columns(level, 1))
+        before = jnp.zeros((CROSS_SHIFT, width), jnp.float32) if chunk == 0 else previous[level]
+        if chunk < chunks - 1:
+            previous[level] = jnp.concatenate([before, upper], axis=0)[-CROSS_SHIFT:]
+        merged = permuted(lower, columns(level, 0)) + delayed(before, upper, columns(level, 2))
+        if level < levels - 1:
+            state[level, 0, span] = merged[:, :rows]
+            state[level, 1, span] = merged[:, rows:]
+            exchange(level + 1, chunk).start()
+        else:
+            final[span] = merged
 
     final = final[...]
     centred = final - jnp.mean(final, axis=0, keepdims=True)

time: 73.5 us -> 65.5 us (0.89)
  the two profiles are of different devices: /device:TPU:1 before, /device:TPU:10 now
where the time goes in v5:
time: 65.5 us; the launch traced here: 65.2 us
  Pallas kernels  63.9 us (98%)
  local copies, waits for them, and re-layouts  1.32 us (2%)
    pallas_call x1, Pallas kernels, subbands(): pl.pallas_call(functools.partial(subband_kernel, n), out_shape=jax.ShapeD...  63.9 us
    unnamed x1, local copies, waits for them, and re-layouts  1.32 us

profile of v5, /device:TPU:10, one launch (start us, length us, event | category | flops | bytes accessed | tf_op | source)
XLA Modules:
  0.0 65.2 jit_solution(7006162468146409375)
XLA Ops:
  0.0 63.9 %subbands.1 = f32[2,8,256]{2,1,0:T(8,128)} custom-call(bf16[2,2,64,16,256]{4,3,2,1,0:T(8,128)(2,1)} %x_hbm.1, f32[192,256]{1,0:T(8,128)} %constant.2.clone.w_hbm, s32[256,1024]{1,0:T(8,128)} %delay_hbm.1, s32[3,4,256]{2,1,0:T(4,128)} %bitcast.1), custom_call_target="tpu_custom_call" | custom-call | tf_op jit(solution)/shard_map/subbands/pallas_call | solution.py:307
  63.9 1.3 %copy.6 = f32[2,8,256]{2,1,0:T(8,128)} copy(f32[2,8,256]{2,1,0:T(8,128)} %subbands.1) | data formatting | bytes 32768

commit v6 on v5

--- a/solution.py
+++ b/solution.py
@@ -230,7 +230,7 @@
         chosen = jnp.where(chosen, 1.0, 0.0).astype(jnp.bfloat16)
         local_delays[group] = jnp.dot(
             delays, chosen, preferred_element_type=jnp.float32
-        ).astype(jnp.int32)
+        ).astype(jnp.bfloat16)
 
     time = lax.broadcasted_iota(jnp.int32, (depth, width), 1) % samples
     inside = lax.broadcasted_iota(jnp.int32, (rows, width), 1) % samples >= STRIDE
@@ -247,11 +247,12 @@
         part[...] = jnp.zeros_like(part)
 
         def horner(step, carry):
-            base = SHIFTS - STRIDE - STRIDE * step
+            base = (SHIFTS - STRIDE - STRIDE * step).astype(jnp.float32)
+            one, zero = jnp.bfloat16(1.0), jnp.bfloat16(0.0)
             group_delays = local_delays[group]
             onehot = jnp.concatenate(
                 [
-                    jnp.where(group_delays == base + shift, 1.0, 0.0).astype(jnp.bfloat16)
+                    jnp.where(group_delays == (base + shift).astype(jnp.bfloat16), one, zero)
                     for shift in range(STRIDE)
                 ],
                 axis=1,
@@ -318,7 +319,7 @@
             pltpu.VMEM((levels, 3, rows), jnp.int32),
             pltpu.VMEM((n, each, upchan, width), jnp.bfloat16),
             pltpu.VMEM((n, each, upchan, width), jnp.bfloat16),
-            pltpu.VMEM((n // members, rows, depth), jnp.int32),
+            pltpu.VMEM((n // members, rows, depth), jnp.bfloat16),
             pltpu.VMEM((STRIDE * depth, width), jnp.bfloat16),
             pltpu.VMEM((rows, width), jnp.float32),
             pltpu.VMEM((rows, width), jnp.float32),

time: 65.5 us -> 65.4 us (level)
  the two profiles are of different devices: /device:TPU:10 before, /device:TPU:14 now
where the time goes in v6:
time: 65.4 us; the launch traced here: 65.1 us
  Pallas kernels  63.8 us (98%)
  local copies, waits for them, and re-layouts  1.32 us (2%)
    pallas_call x1, Pallas kernels, subbands(): pl.pallas_call(functools.partial(subband_kernel, n), out_shape=jax.ShapeD...  63.8 us
    unnamed x1, local copies, waits for them, and re-layouts  1.32 us

profile of v6, /device:TPU:14, one launch (start us, length us, event | category | flops | bytes accessed | tf_op | source)
XLA Modules:
  0.0 65.1 jit_solution(10287324476749229886)
XLA Ops:
  0.0 63.8 %subbands.1 = f32[2,8,256]{2,1,0:T(8,128)} custom-call(bf16[2,2,64,16,256]{4,3,2,1,0:T(8,128)(2,1)} %x_hbm.1, f32[192,256]{1,0:T(8,128)} %constant.2.clone.w_hbm, s32[256,1024]{1,0:T(8,128)} %delay_hbm.1, s32[3,4,256]{2,1,0:T(4,128)} %bitcast.1), custom_call_target="tpu_custom_call" | custom-call | tf_op jit(solution)/shard_map/subbands/pallas_call | solution.py:308
  63.8 1.3 %copy.6 = f32[2,8,256]{2,1,0:T(8,128)} copy(f32[2,8,256]{2,1,0:T(8,128)} %subbands.1) | data formatting | bytes 32768
